TPU v7x, 32 devices: a whole 2x2x4 slice. The times are simulated.
32 devices in a mesh: group: 2 (over y), wide: 8 (over z, x), narrow: 2 (over core).
Axes of the slice: x: 2, y: 2, z: 4, core: 2. Of those that a mesh axis runs over, the one named last changes fastest.
Arguments:
- tokens: bfloat16 [32, 8192], P(('group', 'wide'), 'narrow'), parts along dimension 0, may hold values from -6 to 6
- up_weight: bfloat16 [8192, 2048], P('narrow', 'wide'), may hold values from -0.0625 to 0.0625
- down_weight: bfloat16 [2048, 8192], P('wide', 'narrow'), may hold values from -0.25 to 0.25
- active_blocks: int32 [4, 4], P('group'), parts along dimension 0, may hold values from 0 to 15, as said below
Outputs:
- mixed: bfloat16 [32, 8192], P(('group', 'wide'), 'narrow'), parts along dimension 0
There are 2 independent parts, one for each index of `group`. A program takes and returns all parts, laid end to end along the dimension named above; an argument that names none is the same for every part. Nothing has to cross between parts.
Inputs may be any that keep to these rules, and one draw needn't show every extreme that they name: `active_blocks`: each row names 4 different blocks; some blocks are active in far more tiles than others.
All inputs are finite; a program needn't handle non-finite values.
Results may differ from a plain program's by a relative error of at most 0.005.
Values may be sent and summed in bfloat16 or wider, within the bound.
A program may use at most 64 MiB of HBM per device.

v0:
```python
import jax
import jax.numpy as jnp
from jax import lax
from jax.sharding import PartitionSpec as P

BLOCK = 128


def project_rows(weight, shard_rows):
    return jnp.dot(shard_rows, weight, preferred_element_type=jnp.float32)


def body(tokens, up_weight, down_weight, active_blocks):
    local_cols = up_weight.shape[1]
    local_blocks = local_cols // BLOCK
    partial_value = project_rows(up_weight, lax.all_gather(tokens, "wide", axis=0, tiled=True))
    total_rows = partial_value.shape[0]
    tile_count = active_blocks.shape[0]
    first_block = lax.axis_index("wide") * local_blocks
    owned = first_block + jnp.arange(local_blocks, dtype=jnp.int32)
    flags = jnp.any(active_blocks[:, :, None] == owned[None, None, :], axis=1)
    keeper = jnp.broadcast_to(
        flags[:, None, :, None], (tile_count, total_rows // tile_count, local_blocks, BLOCK)
    ).reshape(total_rows, local_cols)
    unit_sum = lax.psum(partial_value, "narrow")
    hidden = jnp.where(keeper, jax.nn.silu(unit_sum), jnp.float32(0.0)).astype(jnp.bfloat16)
    mixed = lax.psum_scatter(
        jnp.dot(hidden, down_weight, preferred_element_type=jnp.float32),
        "wide",
        scatter_dimension=0,
        tiled=True,
    )
    return mixed.astype(jnp.bfloat16)


def solution(mesh):
    in_specs = (
        P(("group", "wide"), "narrow"),
        P("narrow", "wide"),
        P("wide", "narrow"),
        P("group", None),
    )
    out_specs = P(("group", "wide"), "narrow")
    return jax.shard_map(body, mesh=mesh, in_specs=in_specs, out_specs=out_specs, check_vma=False)
```

profile of v0, /device:TPU:0, one launch (start us, length us, event | category | flops | bytes accessed | tf_op | source)
XLA Modules:
  0.0 80.9 jit_solution(10200851139271329923)
XLA Ops:
  0.0 0.0 copy-start
  0.0 0.0 copy-start.1
  0.0 32.6 %all-gather = bf16[8,2,4096]{2,1,0:T(2,128)(2,1)S(1)} all-gather(bf16[1,2,4096]{2,1,0:T(2,128)(2,1)} %bitcast.8), channel_id=1, replica_groups=mesh['group'=2,'wide'=8,'narrow'=2] {'wide'}, dimensions={0}, use_global_device_ids=true | all-gather | bytes 147456 | tf_op jit(solution)/shard_map/all_gather | solution.py:16
  32.6 0.1 reshape.11
  32.7 0.0 copy-start.2
  32.7 2.0 %fusion.6 = f32[16,256]{1,0:T(8,128)S(1)} fusion(bf16[16,4096]{1,0:T(8,128)(2,1)S(1)} %reshape.11, bf16[4096,256]{1,0:T(8,128)(2,1)} %param.5), kind=kOutput, calls=%fused_computation.10 | convolution fusion | flops 33554432 | bytes 2244608 | tf_op jit(solution)/shard_map/dot_general | solution.py:10
  34.7 3.4 %psum.7 = f32[16,256]{1,0:T(8,128)S(1)} all-reduce(f32[16,256]{1,0:T(8,128)S(1)} %fusion.6), channel_id=1, replica_groups=mesh['group'=2,'wide'=8,'narrow'=2] {'narrow'}, use_global_device_ids=true, to_apply=%region_1.0 | all-reduce | flops 4096 | bytes 32768 | tf_op jit(solution)/shard_map/psum | solution.py:25
  38.1 0.0 copy-done.1
  38.1 0.1 compare_reduce_fusion
  38.2 0.0 copy-done
  38.2 0.4 fusion
  38.6 40.4 %all-reduce.2 = bf16[16,4096]{1,0:T(8,128)(2,1)S(1)} all-reduce(f32[16,4096]{1,0:T(8,128)S(1)} %fusion), channel_id=2, replica_groups=mesh['group'=2,'wide'=8,'narrow'=2] {'wide'}, use_global_device_ids=true, to_apply=%region_2.3.clone | all-reduce | flops 65536 | bytes 393216
  79.0 0.0 copy-done.2
  79.0 0.6 dynamic-slice
  80.2 0.6 dynamic-slice_convert_fusion
  (1 shorter events, 0.0 us)
Async XLA Ops:
  0.0 38.2 %copy-start = (bf16[256,4096]{1,0:T(8,128)(2,1)S(1)}, bf16[256,4096]{1,0:T(8,128)(2,1)}, u32[]{:S(2)}) copy-start(bf16[256,4096]{1,0:T(8,128)(2,1)} %param.6) | copy-start | bytes 6291460
  0.0 38.1 %copy-start.1 = (s32[2,4]{1,0:T(2,128)S(1)}, s32[2,4]{1,0:T(2,128)}, u32[]{:S(2)}) copy-start(s32[2,4]{1,0:T(2,128)} %param.7) | copy-start | bytes 100
  32.7 46.3 %copy-start.2 = (u32[32]{0:T(128)S(1)}, u32[32]{0:T(128)}, u32[]{:S(2)}) copy-start(u32[32]{0:T(128)} %constant.18) | copy-start | bytes 388
where the time goes:
time: 81.1 us; the launch traced here: 80.9 us
  blocking collectives  76.4 us (94%)
  matrix products  2.4 us (3%)
  local copies, waits for them, and re-layouts  1.28 us (2%)
    unnamed x1, blocking collectives  40.4 us
    all_gather x1, blocking collectives, body(): lax.all_gather(tokens, 'wide', axis=0, tiled=True)  32.6 us
    psum x1, blocking collectives, body(): unit_sum = lax.psum(partial_value, 'narrow')  3.36 us
    dot_general x1, matrix products, project_rows(): return jnp.dot(shard_rows, weight, preferred_element_type=jnp.float32)  1.98 us

commit v1 on v0

v1 whole, which is shorter than its diff:
```python
import functools

import jax
import jax.numpy as jnp
from jax import lax
from jax.experimental import pallas as pl
from jax.experimental.pallas import tpu as pltpu
from jax.sharding import PartitionSpec as P

BLOCK = 128
CHUNKS = 2
MESH = pl.DeviceIdType.MESH


def loop(count, step):
    lax.fori_loop(0, count, lambda i, c: (step(i), c)[1], 0, unroll=count <= 8)


def kernel(
    n, tok_hbm, up_hbm, down_hbm, act_hbm, out_ref,
    slots, up, down, act, xf, part, other, sbuf, rslots,
    load_sem, gsend, grecv, nsend, nrecv, rsend, rrecv,
):
    me = lax.axis_index("wide")
    core = lax.axis_index("narrow")
    mate = {"narrow": 1 - core}
    own = tok_hbm.shape[0]
    rows = n * own
    tiles = act_hbm.shape[0]
    width = down_hbm.shape[1]
    chunk = width // CHUNKS

    tok_in = pltpu.make_async_copy(tok_hbm, slots.at[me], load_sem.at[0])
    act_in = pltpu.make_async_copy(act_hbm, act, load_sem.at[1])
    up_in = pltpu.make_async_copy(up_hbm, up, load_sem.at[2])
    down_in = pltpu.make_async_copy(down_hbm, down, load_sem.at[3])
    tok_in.start()

    barrier = pltpu.get_barrier_semaphore()

    def greet(i):
        pl.semaphore_signal(
            barrier, inc=1, device_id={"wide": lax.rem(me + 1 + i, n)}, device_id_type=MESH
        )

    loop(n - 1, greet)
    pl.semaphore_signal(barrier, inc=1, device_id=mate, device_id_type=MESH)
    up_in.start()
    act_in.start()
    down_in.start()
    tok_in.wait()
    pl.semaphore_wait(barrier, n)

    def send_tokens(i):
        pltpu.make_async_remote_copy(
            src_ref=slots.at[me], dst_ref=slots.at[me], send_sem=gsend, recv_sem=grecv,
            device_id={"wide": lax.rem(me + 1 + i, n)}, device_id_type=MESH,
        ).start()

    loop(n - 1, send_tokens)

    act_in.wait()
    masks = []
    for b in range(up.shape[1] // BLOCK):
        block = me * (up.shape[1] // BLOCK) + b
        flag = jnp.max((act[...] == block).astype(jnp.float32), axis=1, keepdims=True)
        flag = jnp.broadcast_to(flag, (tiles, BLOCK))
        masks.append(
            jnp.broadcast_to(flag[:, None, :], (tiles, rows // tiles, BLOCK)).reshape(rows, BLOCK)
        )
    keeper = jnp.concatenate(masks, axis=1)

    up_in.wait()
    most = slots.at[pl.ds(0, n - 1)]
    pltpu.make_async_copy(most, most, grecv).wait()

    for j in range(n):
        xf[j * own : (j + 1) * own, :] = slots[j].astype(jnp.float32)
    part[...] = jnp.dot(
        xf[...].astype(jnp.bfloat16), up[...], preferred_element_type=jnp.float32
    )
    swap = pltpu.make_async_remote_copy(
        src_ref=part, dst_ref=other, send_sem=nsend, recv_sem=nrecv,
        device_id=mate, device_id_type=MESH,
    )
    swap.start()
    down_in.wait()
    swap.wait_recv()
    total = part[...] + other[...]
    hidden = jnp.where(keeper > 0.0, total / (1.0 + jnp.exp(-total)), 0.0).astype(jnp.bfloat16)

    for c in range(CHUNKS):
        cols = pl.ds(c * chunk, chunk)
        mix = jnp.dot(hidden, down[:, cols], preferred_element_type=jnp.float32)
        for j in range(n):
            sbuf[j, :, cols] = mix[j * own : (j + 1) * own].astype(jnp.bfloat16)

        def send_part(i):
            peer = lax.rem(me + 1 + i, n)
            pltpu.make_async_remote_copy(
                src_ref=sbuf.at[peer, :, cols], dst_ref=rslots.at[i, :, cols],
                send_sem=rsend.at[c], recv_sem=rrecv.at[c],
                device_id={"wide": peer}, device_id_type=MESH,
            ).start()

        loop(n - 1, send_part)

    for c in range(CHUNKS):
        cols = pl.ds(c * chunk, chunk)
        got = rslots.at[:, :, cols]
        pltpu.make_async_copy(got, got, rrecv.at[c]).wait()
        out_ref[:, cols] = lax.fori_loop(
            0, n - 1, lambda i, s: s + rslots[i, :, cols].astype(jnp.float32),
            sbuf[me, :, cols].astype(jnp.float32), unroll=n <= 8,
        ).astype(out_ref.dtype)

    pltpu.make_async_copy(most, most, gsend).wait()
    swap.wait_send()
    for c in range(CHUNKS):
        sent = rslots.at[:, :, pl.ds(c * chunk, chunk)]
        pltpu.make_async_copy(sent, sent, rsend.at[c]).wait()


def body(n, tokens, up_weight, down_weight, active_blocks):
    own, width = tokens.shape
    rows = n * own
    local = up_weight.shape[1]
    dma = pltpu.SemaphoreType.DMA
    return pl.pallas_call(
        functools.partial(kernel, n),
        out_shape=jax.ShapeDtypeStruct((own, width), jnp.bfloat16),
        in_specs=[pl.BlockSpec(memory_space=pltpu.HBM)] * 4,
        out_specs=pl.BlockSpec(memory_space=pltpu.VMEM),
        scratch_shapes=[
            pltpu.VMEM((n, own, width), jnp.bfloat16),
            pltpu.VMEM(up_weight.shape, jnp.bfloat16),
            pltpu.VMEM(down_weight.shape, jnp.bfloat16),
            pltpu.VMEM(active_blocks.shape, jnp.int32),
            pltpu.VMEM((rows, width), jnp.float32),
            pltpu.VMEM((rows, local), jnp.float32),
            pltpu.VMEM((rows, local), jnp.float32),
            pltpu.VMEM((n, own, width), jnp.bfloat16),
            pltpu.VMEM((n - 1, own, width), jnp.bfloat16),
            dma((4,)), dma, dma, dma, dma, dma((CHUNKS,)), dma((CHUNKS,)),
        ],
        compiler_params=pltpu.CompilerParams(
            collective_id=0, has_side_effects=True, vmem_limit_bytes=64 * 1024 * 1024 - 65536
        ),
    )(tokens, up_weight, down_weight, active_blocks)


def solution(mesh):
    in_specs = (
        P(("group", "wide"), "narrow"),
        P("narrow", "wide"),
        P("wide", "narrow"),
        P("group", None),
    )
    out_specs = P(("group", "wide"), "narrow")
    return jax.shard_map(
        functools.partial(body, mesh.shape["wide"]),
        mesh=mesh, in_specs=in_specs, out_specs=out_specs, check_vma=False,
    )
```

time: 81.1 us -> 19.5 us (0.24)
  the two profiles are of different devices: /device:TPU:0 before, /device:TPU:1 now
where the time goes in v1:
time: 19.5 us; the launch traced here: 19.1 us
  Pallas kernels  17.8 us (91%)
  local copies, waits for them, and re-layouts  1.34 us (7%)
    pallas_call x1, Pallas kernels, body(): pl.pallas_call(functools.partial(kernel, n), out_shape=jax.ShapeDtypeStru...  17.8 us
    unnamed x1, local copies, waits for them, and re-layouts  1.34 us

profile of v1, /device:TPU:1, one launch (start us, length us, event | category | flops | bytes accessed | tf_op | source)
XLA Modules:
  0.0 19.1 jit_solution(17732401811237535606)
XLA Ops:
  0.0 17.8 %shard_map.46 = bf16[2,4096]{1,0:T(2,128)(2,1)} custom-call(bf16[2,4096]{1,0:T(2,128)(2,1)} %tok_hbm.1, bf16[4096,256]{1,0:T(8,128)(2,1)} %up_hbm.1, bf16[256,4096]{1,0:T(8,128)(2,1)} %down_hbm.1, s32[2,4]{1,0:T(2,128)} %act_hbm.1), custom_call_target="tpu_custom_call" | custom-call | tf_op jit(solution)/shard_map/pallas_call | solution.py:129
  17.8 1.3 %copy.6 = bf16[2,4096]{1,0:T(2,128)(2,1)} copy(bf16[2,4096]{1,0:T(2,128)(2,1)} %shard_map.46) | data formatting | bytes 32768

commit v2 on v1

--- a/solution.py
+++ b/solution.py
@@ -8,17 +8,21 @@
 from jax.sharding import PartitionSpec as P
 
 BLOCK = 128
-CHUNKS = 2
+CHUNKS = 1
 MESH = pl.DeviceIdType.MESH
 
 
 def loop(count, step):
-    lax.fori_loop(0, count, lambda i, c: (step(i), c)[1], 0, unroll=count <= 8)
+    if count <= 8:
+        for i in range(count):
+            step(i)
+        return
+    lax.fori_loop(0, count, lambda i, c: (step(i), c)[1], 0)
 
 
 def kernel(
-    n, tok_hbm, up_hbm, down_hbm, act_hbm, out_ref,
-    slots, up, down, act, xf, part, other, sbuf, rslots,
+    n, tok_hbm, up_hbm, down_hbm, act_hbm, rslots,
+    slots, up, down, act, xf, part, other, sbuf,
     load_sem, gsend, grecv, nsend, nrecv, rsend, rrecv,
 ):
     me = lax.axis_index("wide")
@@ -30,6 +34,13 @@
     width = down_hbm.shape[1]
     chunk = width // CHUNKS
 
+    def flip(d):
+        bits = [lax.rem(me // 2**k, 2) for k in range(3)]
+        return sum((1 - b if d // 2**k % 2 else b) * 2**k for k, b in enumerate(bits))
+
+    def partner(i):
+        return flip(n - 1 - i) if n == 8 else lax.rem(me + 1 + i, n)
+
     tok_in = pltpu.make_async_copy(tok_hbm, slots.at[me], load_sem.at[0])
     act_in = pltpu.make_async_copy(act_hbm, act, load_sem.at[1])
     up_in = pltpu.make_async_copy(up_hbm, up, load_sem.at[2])
@@ -40,7 +51,7 @@
 
     def greet(i):
         pl.semaphore_signal(
-            barrier, inc=1, device_id={"wide": lax.rem(me + 1 + i, n)}, device_id_type=MESH
+            barrier, inc=1, device_id={"wide": partner(i)}, device_id_type=MESH
         )
 
     loop(n - 1, greet)
@@ -54,7 +65,7 @@
     def send_tokens(i):
         pltpu.make_async_remote_copy(
             src_ref=slots.at[me], dst_ref=slots.at[me], send_sem=gsend, recv_sem=grecv,
-            device_id={"wide": lax.rem(me + 1 + i, n)}, device_id_type=MESH,
+            device_id={"wide": partner(i)}, device_id_type=MESH,
         ).start()
 
     loop(n - 1, send_tokens)
@@ -96,7 +107,7 @@
             sbuf[j, :, cols] = mix[j * own : (j + 1) * own].astype(jnp.bfloat16)
 
         def send_part(i):
-            peer = lax.rem(me + 1 + i, n)
+            peer = partner(i)
             pltpu.make_async_remote_copy(
                 src_ref=sbuf.at[peer, :, cols], dst_ref=rslots.at[i, :, cols],
                 send_sem=rsend.at[c], recv_sem=rrecv.at[c],
@@ -105,19 +116,17 @@
 
         loop(n - 1, send_part)
 
+    keep = pltpu.make_async_copy(sbuf.at[me], rslots.at[n - 1], load_sem.at[0])
+    keep.start()
     for c in range(CHUNKS):
         cols = pl.ds(c * chunk, chunk)
-        got = rslots.at[:, :, cols]
+        got = rslots.at[pl.ds(0, n - 1), :, cols]
         pltpu.make_async_copy(got, got, rrecv.at[c]).wait()
-        out_ref[:, cols] = lax.fori_loop(
-            0, n - 1, lambda i, s: s + rslots[i, :, cols].astype(jnp.float32),
-            sbuf[me, :, cols].astype(jnp.float32), unroll=n <= 8,
-        ).astype(out_ref.dtype)
-
     pltpu.make_async_copy(most, most, gsend).wait()
     swap.wait_send()
+    keep.wait()
     for c in range(CHUNKS):
-        sent = rslots.at[:, :, pl.ds(c * chunk, chunk)]
+        sent = rslots.at[pl.ds(0, n - 1), :, pl.ds(c * chunk, chunk)]
         pltpu.make_async_copy(sent, sent, rsend.at[c]).wait()
 
 
@@ -126,11 +135,11 @@
     rows = n * own
     local = up_weight.shape[1]
     dma = pltpu.SemaphoreType.DMA
-    return pl.pallas_call(
+    terms = pl.pallas_call(
         functools.partial(kernel, n),
-        out_shape=jax.ShapeDtypeStruct((own, width), jnp.bfloat16),
+        out_shape=jax.ShapeDtypeStruct((n, own, width), jnp.bfloat16),
         in_specs=[pl.BlockSpec(memory_space=pltpu.HBM)] * 4,
-        out_specs=pl.BlockSpec(memory_space=pltpu.VMEM),
+        out_specs=pl.BlockSpec(memory_space=pltpu.HBM),
         scratch_shapes=[
             pltpu.VMEM((n, own, width), jnp.bfloat16),
             pltpu.VMEM(up_weight.shape, jnp.bfloat16),
@@ -140,13 +149,13 @@
             pltpu.VMEM((rows, local), jnp.float32),
             pltpu.VMEM((rows, local), jnp.float32),
             pltpu.VMEM((n, own, width), jnp.bfloat16),
-            pltpu.VMEM((n - 1, own, width), jnp.bfloat16),
             dma((4,)), dma, dma, dma, dma, dma((CHUNKS,)), dma((CHUNKS,)),
         ],
         compiler_params=pltpu.CompilerParams(
             collective_id=0, has_side_effects=True, vmem_limit_bytes=64 * 1024 * 1024 - 65536
         ),
     )(tokens, up_weight, down_weight, active_blocks)
+    return jnp.sum(terms.astype(jnp.float32), axis=0).astype(jnp.bfloat16)
 
 
 def solution(mesh):

time: 19.5 us -> 18.3 us (0.938)
  the two profiles are of different devices: /device:TPU:1 before, /device:TPU:0 now
where the time goes in v2:
time: 18.3 us; the launch traced here: 18 us
  Pallas kernels  16.4 us (90%)
  other arithmetic  1.64 us (9%)
    pallas_call x1, Pallas kernels, body(): pl.pallas_call(functools.partial(kernel, n), out_shape=jax.ShapeDtypeStru...  16.4 us
    reduce_sum x1, other arithmetic, body(): return jnp.sum(terms.astype(jnp.float32), axis=0).astype(jnp.bfloat16)  1.64 us

profile of v2, /device:TPU:0, one launch (start us, length us, event | category | flops | bytes accessed | tf_op | source)
XLA Modules:
  0.0 18.0 jit_solution(1303025425176657927)
XLA Ops:
  0.0 16.4 %shard_map.46 = bf16[8,2,4096]{2,1,0:T(2,128)(2,1)} custom-call(bf16[2,4096]{1,0:T(2,128)(2,1)} %tok_hbm.1, bf16[4096,256]{1,0:T(8,128)(2,1)} %up_hbm.1, bf16[256,4096]{1,0:T(8,128)(2,1)} %down_hbm.1, s32[2,4]{1,0:T(2,128)} %act_hbm.1), custom_call_target="tpu_custom_call" | custom-call | tf_op jit(solution)/shard_map/pallas_call | solution.py:138
  16.4 1.6 %reduce_sum.12 = bf16[2,4096]{1,0:T(2,128)(2,1)} reduce(bf16[8,2,4096]{2,1,0:T(2,128)(2,1)} %shard_map.46, bf16[]{:T(256)} %constant.2.clone.1), dimensions={0}, to_apply=%region_0.0 | reduce | flops 57344 | bytes 147458 | tf_op jit(solution)/shard_map/reduce_sum | solution.py:158

commit v3 on v2

--- a/solution.py
+++ b/solution.py
@@ -27,19 +27,23 @@
 ):
     me = lax.axis_index("wide")
     core = lax.axis_index("narrow")
-    mate = {"narrow": 1 - core}
+    group = lax.axis_index("group")
+    mate = (group, me, 1 - core)
     own = tok_hbm.shape[0]
     rows = n * own
     tiles = act_hbm.shape[0]
     width = down_hbm.shape[1]
     chunk = width // CHUNKS
 
+    bits = [lax.rem(me // 2**k, 2) for k in range(3)]
+
     def flip(d):
-        bits = [lax.rem(me // 2**k, 2) for k in range(3)]
         return sum((1 - b if d // 2**k % 2 else b) * 2**k for k, b in enumerate(bits))
 
+    peers = [flip(n - 1 - i) for i in range(n - 1)] if n == 8 else None
+
     def partner(i):
-        return flip(n - 1 - i) if n == 8 else lax.rem(me + 1 + i, n)
+        return peers[i] if n == 8 else lax.rem(me + 1 + i, n)
 
     tok_in = pltpu.make_async_copy(tok_hbm, slots.at[me], load_sem.at[0])
     act_in = pltpu.make_async_copy(act_hbm, act, load_sem.at[1])
@@ -51,7 +55,7 @@
 
     def greet(i):
         pl.semaphore_signal(
-            barrier, inc=1, device_id={"wide": partner(i)}, device_id_type=MESH
+            barrier, inc=1, device_id=(group, partner(i), core), device_id_type=MESH
         )
 
     loop(n - 1, greet)
@@ -65,7 +69,7 @@
     def send_tokens(i):
         pltpu.make_async_remote_copy(
             src_ref=slots.at[me], dst_ref=slots.at[me], send_sem=gsend, recv_sem=grecv,
-            device_id={"wide": partner(i)}, device_id_type=MESH,
+            device_id=(group, partner(i), core), device_id_type=MESH,
         ).start()
 
     loop(n - 1, send_tokens)
@@ -76,54 +80,79 @@
         block = me * (up.shape[1] // BLOCK) + b
         flag = jnp.max((act[...] == block).astype(jnp.float32), axis=1, keepdims=True)
         flag = jnp.broadcast_to(flag, (tiles, BLOCK))
-        masks.append(
-            jnp.broadcast_to(flag[:, None, :], (tiles, rows // tiles, BLOCK)).reshape(rows, BLOCK)
-        )
+        if n == 8:
+            tall = rows // tiles
+            place = lax.broadcasted_iota(jnp.int32, (rows, BLOCK), 0) // own
+            owner = jnp.where(place == n - 1, me, 0)
+            for i, peer in enumerate(peers):
+                owner = jnp.where(place == i, peer, owner)
+            row = owner * own + lax.broadcasted_iota(jnp.int32, (rows, BLOCK), 0) % own
+            mask = jnp.zeros((rows, BLOCK), jnp.float32)
+            for t in range(tiles):
+                mask = jnp.where(row // tall == t, flag[t : t + 1], mask)
+            masks.append(mask)
+        else:
+            masks.append(
+                jnp.broadcast_to(flag[:, None, :], (tiles, rows // tiles, BLOCK)).reshape(rows, BLOCK)
+            )
     keeper = jnp.concatenate(masks, axis=1)
 
     up_in.wait()
     most = slots.at[pl.ds(0, n - 1)]
     pltpu.make_async_copy(most, most, grecv).wait()
 
-    for j in range(n):
-        xf[j * own : (j + 1) * own, :] = slots[j].astype(jnp.float32)
-    part[...] = jnp.dot(
-        xf[...].astype(jnp.bfloat16), up[...], preferred_element_type=jnp.float32
-    )
-    swap = pltpu.make_async_remote_copy(
-        src_ref=part, dst_ref=other, send_sem=nsend, recv_sem=nrecv,
-        device_id=mate, device_id_type=MESH,
-    )
-    swap.start()
+    ranks = [*peers, me] if n == 8 else list(range(n))
+    for j, owner in enumerate(ranks):
+        xf[j * own : (j + 1) * own, :] = slots[owner].astype(jnp.float32)
+    half = up.shape[1] // 2
+    swaps = []
+    for k in range(2):
+        part[k] = jnp.dot(
+            xf[...].astype(jnp.bfloat16), up[:, k * half : (k + 1) * half],
+            preferred_element_type=jnp.float32,
+        )
+        swap = pltpu.make_async_remote_copy(
+            src_ref=part.at[k], dst_ref=other.at[k], send_sem=nsend.at[k], recv_sem=nrecv.at[k],
+            device_id=mate, device_id_type=MESH,
+        )
+        swap.start()
+        swaps.append(swap)
     down_in.wait()
-    swap.wait_recv()
-    total = part[...] + other[...]
-    hidden = jnp.where(keeper > 0.0, total / (1.0 + jnp.exp(-total)), 0.0).astype(jnp.bfloat16)
+    parts = []
+    for k in range(2):
+        swaps[k].wait_recv()
+        total = part[k] + other[k]
+        active = keeper[:, k * half : (k + 1) * half] > 0.0
+        parts.append(jnp.where(active, total / (1.0 + jnp.exp(-total)), 0.0).astype(jnp.bfloat16))
+    hidden = jnp.concatenate(parts, axis=1)
 
     for c in range(CHUNKS):
         cols = pl.ds(c * chunk, chunk)
         mix = jnp.dot(hidden, down[:, cols], preferred_element_type=jnp.float32)
-        for j in range(n):
+        for j in range(n - 1 if n == 8 else 0, n):
             sbuf[j, :, cols] = mix[j * own : (j + 1) * own].astype(jnp.bfloat16)
 
         def send_part(i):
             peer = partner(i)
+            if n == 8:
+                sbuf[i, :, cols] = mix[i * own : (i + 1) * own].astype(jnp.bfloat16)
             pltpu.make_async_remote_copy(
-                src_ref=sbuf.at[peer, :, cols], dst_ref=rslots.at[i, :, cols],
+                src_ref=sbuf.at[i if n == 8 else peer, :, cols], dst_ref=rslots.at[i, :, cols],
                 send_sem=rsend.at[c], recv_sem=rrecv.at[c],
-                device_id={"wide": peer}, device_id_type=MESH,
+                device_id=(group, peer, core), device_id_type=MESH,
             ).start()
 
         loop(n - 1, send_part)
 
-    keep = pltpu.make_async_copy(sbuf.at[me], rslots.at[n - 1], load_sem.at[0])
+    pltpu.make_async_copy(most, most, gsend).wait()
+    for swap in swaps:
+        swap.wait_send()
+    keep = pltpu.make_async_copy(sbuf.at[n - 1 if n == 8 else me], rslots.at[n - 1], load_sem.at[0])
     keep.start()
     for c in range(CHUNKS):
         cols = pl.ds(c * chunk, chunk)
         got = rslots.at[pl.ds(0, n - 1), :, cols]
         pltpu.make_async_copy(got, got, rrecv.at[c]).wait()
-    pltpu.make_async_copy(most, most, gsend).wait()
-    swap.wait_send()
     keep.wait()
     for c in range(CHUNKS):
         sent = rslots.at[pl.ds(0, n - 1), :, pl.ds(c * chunk, chunk)]
@@ -146,10 +175,10 @@
             pltpu.VMEM(down_weight.shape, jnp.bfloat16),
             pltpu.VMEM(active_blocks.shape, jnp.int32),
             pltpu.VMEM((rows, width), jnp.float32),
-            pltpu.VMEM((rows, local), jnp.float32),
-            pltpu.VMEM((rows, local), jnp.float32),
+            pltpu.VMEM((2, rows, local // 2), jnp.float32),
+            pltpu.VMEM((2, rows, local // 2), jnp.float32),
             pltpu.VMEM((n, own, width), jnp.bfloat16),
-            dma((4,)), dma, dma, dma, dma, dma((CHUNKS,)), dma((CHUNKS,)),
+            dma((4,)), dma, dma, dma((2,)), dma((2,)), dma((CHUNKS,)), dma((CHUNKS,)),
         ],
         compiler_params=pltpu.CompilerParams(
             collective_id=0, has_side_effects=True, vmem_limit_bytes=64 * 1024 * 1024 - 65536

time: 18.3 us -> 17.9 us (0.978)
  Pallas kernels: 16.4 us -> 16 us
    pallas_call x1, Pallas kernels: 16.4 us -> 16 us  [body(): pl.pallas_call(functools.partial(kernel, n), out_shape=jax.ShapeDtypeStru...]
where the time goes in v3:
time: 17.9 us; the launch traced here: 17.7 us
  Pallas kernels  16 us (89%)
  other arithmetic  1.64 us (9%)
    pallas_call x1, Pallas kernels, body(): pl.pallas_call(functools.partial(kernel, n), out_shape=jax.ShapeDtypeStru...  16 us
    reduce_sum x1, other arithmetic, body(): return jnp.sum(terms.astype(jnp.float32), axis=0).astype(jnp.bfloat16)  1.64 us

profile of v3, /device:TPU:0, one launch (start us, length us, event | category | flops | bytes accessed | tf_op | source)
XLA Modules:
  0.0 17.7 jit_solution(1036454639193496546)
XLA Ops:
  0.0 16.0 %shard_map.46 = bf16[8,2,4096]{2,1,0:T(2,128)(2,1)} custom-call(bf16[2,4096]{1,0:T(2,128)(2,1)} %tok_hbm.1, bf16[4096,256]{1,0:T(8,128)(2,1)} %up_hbm.1, bf16[256,4096]{1,0:T(8,128)(2,1)} %down_hbm.1, s32[2,4]{1,0:T(2,128)} %act_hbm.1), custom_call_target="tpu_custom_call" | custom-call | tf_op jit(solution)/shard_map/pallas_call | solution.py:167
  16.0 1.6 %reduce_sum.12 = bf16[2,4096]{1,0:T(2,128)(2,1)} reduce(bf16[8,2,4096]{2,1,0:T(2,128)(2,1)} %shard_map.46, bf16[]{:T(256)} %constant.2.clone.1), dimensions={0}, to_apply=%region_0.0 | reduce | flops 57344 | bytes 147458 | tf_op jit(solution)/shard_map/reduce_sum | solution.py:187
